TPU v7x, 128 devices: a whole 4x4x4 slice. The times are simulated.
128 devices in a mesh: expert: 32 (over z, x, core), dp: 4 (over y).
Axes of the slice: x: 4, y: 4, z: 4, core: 2. Of those that a mesh axis runs over, the one named last changes fastest.
Arguments:
- tokens: bfloat16 [24576, 1024], P(('expert', 'dp')), may hold values from -96 to 96
- out_grad: bfloat16 [24576, 1024], P(('expert', 'dp')), may hold values from -6 to 6
- routes: int32 [24576, 2], P(('expert', 'dp')), may hold values from 0 to 31, all different within a row
- router_weight: float32 [1024, 32], replicated, may hold values from -0.5 to 0.5
- gate_weight: bfloat16 [32, 2816, 1024], P('expert'), may hold values from -0.1875 to 0.1875
- up_weight: bfloat16 [32, 2816, 1024], P('expert'), may hold values from -0.1875 to 0.1875
- down_weight: bfloat16 [32, 2816, 1024], P('expert'), may hold values from -0.109375 to 0.109375
Outputs:
- in_grad: bfloat16 [24576, 1024], P(('expert', 'dp'))
- grad_experts: bfloat16 [32, 2816, 3, 1024], P('expert', 'dp')
- grad_router: float32 [1024, 32], replicated
Inputs may be any that keep to these rules, and one draw needn't show every extreme that they name: `routes`: each row names two different experts, and every expert is named by some row.
All inputs are finite; a program needn't handle non-finite values.
Results may differ from a plain program's by a relative error of at most 0.015.
Values may be sent and summed in bfloat16 or wider, within the bound.
No kernel may reach another device: no remote copies, remote signals or barrier semaphores. Data moves between devices by JAX's collectives and lax.ppermute only.
A program may use at most 192 MiB of HBM per device.

v0:
```python
import functools
import jax
import jax.numpy as jnp
from jax import lax
from jax.experimental import pallas as pl
from jax.experimental.pallas import tpu as pltpu
from jax.sharding import PartitionSpec as P

SQRT_TWO_OVER_PI = 0.7978845608
CUBIC_COEF = 0.044715
STRIDE = 16
F32 = jnp.float32
BF16 = jnp.bfloat16
VMEM_LIMIT = 60 * 1024 * 1024

FEATURE_DIMS = (((1,), (1,)), ((), ()))
ROW_DIMS = (((0,), (0,)), ((), ()))


def dot(left, right, dims=(((1,), (0,)), ((), ()))):
    return lax.dot_general(left, right, dims, preferred_element_type=F32)


def gelu_parts(values):
    square = values * values
    tanh_value = jnp.tanh(values * (SQRT_TWO_OVER_PI + (SQRT_TWO_OVER_PI * CUBIC_COEF) * square))
    half = 0.5 + 0.5 * tanh_value
    slope = half + (half * (1.0 - tanh_value)) * values * (
        SQRT_TWO_OVER_PI + (3.0 * CUBIC_COEF * SQRT_TWO_OVER_PI) * square
    )
    return (values * half, slope)


def split_three(values):
    high = values.astype(BF16)
    rest = values - high.astype(F32)
    mid = rest.astype(BF16)
    low = (rest - mid.astype(F32)).astype(BF16)
    return (high, mid, low)


def softmax(logits, axis):
    shifted = jnp.exp(logits - jnp.max(logits, axis, keepdims=True))
    return shifted / jnp.sum(shifted, axis, keepdims=True)


def slot_rows(routes, experts, capacity):
    count_tok = routes.shape[1]
    expert_ids = lax.broadcasted_iota(jnp.int32, (experts, count_tok), 0)
    first = expert_ids == routes[0:1, :]
    second = expert_ids == routes[1:2, :]
    earlier = (
        lax.broadcasted_iota(jnp.int32, (count_tok, count_tok), 0)
        < lax.broadcasted_iota(jnp.int32, (count_tok, count_tok), 1)
    ).astype(BF16)
    first_hits = first.astype(F32)
    second_hits = second.astype(F32)
    first_before = dot(first_hits.astype(BF16), earlier)
    second_before = dot(second_hits.astype(BF16), earlier) + jnp.sum(first_hits, 1, keepdims=True)
    first_pos = jnp.sum(first_hits * first_before, 0, keepdims=True)
    second_pos = jnp.sum(second_hits * second_before, 0, keepdims=True)
    slots = []
    for pos, route in ((first_pos, routes[0:1, :]), (second_pos, routes[1:2, :])):
        pos = pos.astype(jnp.int32)
        slots.append(jnp.where(pos < capacity, route * STRIDE + pos, -1))
    return slots


def slot_mask(slots, experts):
    count_tok = slots[0].shape[1]
    slot_ids = lax.broadcasted_iota(jnp.int32, (experts * STRIDE, count_tok), 0)
    return ((slot_ids == slots[0]) | (slot_ids == slots[1])).astype(F32).astype(BF16)


def dispatch_kernel(experts, capacity, tokens, out_grad, routes, sent):
    mask = slot_mask(slot_rows(routes[...], experts, capacity), experts)
    for k, source in enumerate((tokens, out_grad)):
        rows = dot(mask, source[...]).astype(BF16).reshape(experts, STRIDE, source.shape[1])
        sent[:, k * STRIDE : (k + 1) * STRIDE, :] = rows


def combine_kernel(experts, capacity, routes, back, after, in_grad, spread, packed):
    rows = back.shape[0]
    spare = lax.broadcasted_iota(jnp.int32, (8, rows), 1) % STRIDE == STRIDE - 1
    sums = dot(spare.astype(F32).astype(BF16), back[...])
    lanes = packed.shape[1]
    for c in range(packed.shape[0]):
        packed[c : c + 1, :] = sums[:1, c * lanes : (c + 1) * lanes]
    spread[...] = jnp.broadcast_to(packed[...][None], spread.shape)
    mask = slot_mask(slot_rows(routes[...], experts, capacity), experts)
    in_grad[...] = dot(mask, back[...], ROW_DIMS).astype(BF16)


def total_kernel(spread, after, grad_router):
    experts = grad_router.shape[0]
    devices, chunks, lanes = spread.shape
    summed = jnp.sum(spread[...].reshape(experts, devices // experts, chunks, lanes), 1)
    for c in range(chunks):
        grad_router[:, c * lanes : (c + 1) * lanes] = summed[:, c, :]


def expert_kernel(tile, tiles, *refs):
    place, router = refs[:2]
    weights = refs[2:5]
    got = refs[5]
    (
        row_grads,
        w_gate,
        w_up,
        w_down,
        total,
        hits,
        even,
        odd,
        arrived,
    ) = refs[-9:]
    held = (w_gate, w_up, w_down)
    rows = hits.shape[0]
    count = router.shape[0]
    lanes = hits.shape[1]

    features = got.shape[3]

    def rows_x():
        return got[:, 0].reshape(rows, features)

    def rows_g():
        return got[:, 1].reshape(rows, features)

    def weight_copies(i):
        part = pl.ds(i * tile, tile)
        return [
            pltpu.make_async_copy(weights[k].at[0, part, :], held[k].at[part, :], arrived.at[k, i])
            for k in range(3)
        ]

    for i in range(tiles):
        for copy in weight_copies(i):
            copy.start()
    total[...] = jnp.zeros_like(total)
    hits[...] = jnp.zeros_like(hits)
    high, mid, low = split_three(router[...])
    parts = dot(rows_x(), jnp.concatenate([high, mid, low], 0), FEATURE_DIMS)
    probs = softmax(parts[:, :count] + parts[:, count : 2 * count] + parts[:, 2 * count :], 1)
    mine = lax.broadcasted_iota(jnp.int32, probs.shape, 1) == place[0]
    gate = jnp.sum(jnp.where(mine, probs, 0.0), 1, keepdims=True)
    gate_wide = jnp.broadcast_to(gate, (rows, tile))

    def wait(i):
        for copy in weight_copies(i):
            copy.wait()

    def part(i):
        return pl.ds(pl.multiple_of(i * tile, tile), tile)

    def before(i, slot):
        slot[0] = dot(rows_x(), w_gate[part(i), :], FEATURE_DIMS)
        slot[1] = dot(rows_x(), w_up[part(i), :], FEATURE_DIMS)
        slot[2] = dot(rows_g(), w_down[part(i), :], FEATURE_DIMS)

    def after(i, slot):
        gelu_value, gelu_slope = gelu_parts(slot[0])
        up_pre = slot[1]
        raw_grad = slot[2]
        hit = gelu_value * up_pre * raw_grad
        hits[...] += sum(hit[:, c : c + lanes] for c in range(0, tile, lanes))
        hidden_grad = raw_grad * gate_wide
        pre_gate_grad = (hidden_grad * up_pre * gelu_slope).astype(BF16)
        pre_up_grad = (hidden_grad * gelu_value).astype(BF16)
        total[...] += dot(pre_gate_grad, w_gate[part(i), :]) + dot(pre_up_grad, w_up[part(i), :])

    wait(0)
    before(0, even)

    def pair(j, carry):
        wait(2 * j + 1)
        wait(2 * j + 2)
        before(2 * j + 1, odd)
        after(2 * j, even)
        before(2 * j + 2, even)
        after(2 * j + 1, odd)
        return carry

    lax.fori_loop(0, (tiles - 1) // 2, pair, 0)
    if tiles % 2 == 0:
        wait(tiles - 1)
        before(tiles - 1, odd)
        after(tiles - 2, even)
        after(tiles - 1, odd)
    else:
        after(tiles - 1, even)

    logit_grads = jnp.sum(hits[...], 1, keepdims=True) * gate * (mine.astype(F32) - probs)
    logit_high = logit_grads.astype(BF16)
    logit_low = (logit_grads - logit_high.astype(F32)).astype(BF16)
    router_part = dot(logit_high, high) + dot(logit_high, mid) + dot(logit_low, high)
    router_term = dot(logit_high, rows_x(), ROW_DIMS) + dot(logit_low, rows_x(), ROW_DIMS)
    spare = (
        lax.broadcasted_iota(jnp.int32, (rows, count), 0)
        == lax.broadcasted_iota(jnp.int32, (rows, count), 1) * STRIDE + STRIDE - 1
    )
    router_rows = dot(spare.astype(F32).astype(BF16), router_term.astype(BF16))
    row_grads[...] = (
        (total[...] + router_part + router_rows).astype(BF16).reshape(row_grads.shape)
    )


def weight_kernel(parts_of, sources_count, first, *refs):
    units = len(parts_of)
    place, router = refs[:2]
    weights = refs[2:5]
    sources = refs[5 : 5 + sources_count]
    before = None if first else refs[-10]
    out, held, even, odd, terms, total, stage, w_sem, o_sem = refs[-9:]
    count = router.shape[0]
    hidden = held.shape[1]
    unit = even.shape[2]
    features = sources[0].shape[3]
    offset = pl.multiple_of(place[1] * hidden, STRIDE)

    def weight_copy(k):
        return pltpu.make_async_copy(
            weights[k].at[0, pl.ds(offset, hidden), :], held.at[k], w_sem.at[k]
        )

    def rows(k, u):
        source, part = parts_of[u]
        size = sources[source].shape[0] // 2
        return sources[source][part * size : (part + 1) * size, k].reshape(unit, features)

    def rows_x(u):
        return rows(0, u)

    def rows_g(u):
        return rows(1, u)

    def out_copy(k):
        return pltpu.make_async_copy(stage.at[k], out.at[k], o_sem.at[k])

    def before_copy(k):
        return pltpu.make_async_copy(before.at[k], total.at[k], o_sem.at[3 + k])

    for k in range(3):
        weight_copy(k).start()
    stacked = jnp.concatenate(split_three(router[...]), 0)
    gates = [None] * units

    def prepare(u, slot):
        if u == 0:
            weight_copy(0).wait()
        slot[0] = dot(held[0], rows_x(u), FEATURE_DIMS)
        if u == 0:
            weight_copy(1).wait()
        slot[1] = dot(held[1], rows_x(u), FEATURE_DIMS)
        parts = dot(stacked, rows_x(u), FEATURE_DIMS)
        probs = softmax(parts[:count] + parts[count : 2 * count] + parts[2 * count :], 0)
        mine = lax.broadcasted_iota(jnp.int32, probs.shape, 0) == place[0]
        gates[u] = jnp.sum(jnp.where(mine, probs, 0.0), 0, keepdims=True)
        if u == 0:
            weight_copy(2).wait()
        if u == 1 and not first:
            for k in range(3):
                before_copy(k).start()
        slot[2] = dot(held[2], rows_g(u), FEATURE_DIMS)

    def finish(u, slot):
        where = slice(u * unit, (u + 1) * unit)
        gelu_value, gelu_slope = gelu_parts(slot[0])
        up_pre = slot[1]
        hidden_grad = slot[2] * gates[u]
        terms[0, :, where] = (hidden_grad * up_pre * gelu_slope).astype(BF16)
        terms[1, :, where] = (hidden_grad * gelu_value).astype(BF16)
        terms[2, :, where] = (gelu_value * up_pre * gates[u]).astype(BF16)

    slots = (even, odd)
    prepare(0, slots[0])
    for u in range(units):
        if u + 1 < units:
            prepare(u + 1, slots[(u + 1) % 2])
        finish(u, slots[u % 2])
    for k in range(3):
        value = None
        for i, source in enumerate(sources):
            count_rows = 2 * unit
            part = dot(
                terms[k, :, i * count_rows : (i + 1) * count_rows],
                source[:, k // 2].reshape(count_rows, features),
            )
            value = part if value is None else value + part
        if not first:
            before_copy(k).wait()
            value = value + total[k].astype(F32)
        stage[k] = value.astype(stage.dtype)
        out_copy(k).start()
    for k in range(3):
        out_copy(k).wait()


def run_dispatch(tokens, out_grad, routes, experts, capacity):
    shape = jax.ShapeDtypeStruct((experts, 2 * STRIDE, tokens.shape[1]), BF16)
    return pl.pallas_call(
        functools.partial(dispatch_kernel, experts, capacity),
        out_shape=shape,
        compiler_params=pltpu.CompilerParams(vmem_limit_bytes=VMEM_LIMIT),
        name="dispatch",
    )(tokens, out_grad, routes)


def run_combine(routes, back, after, experts, capacity, devices):
    vmem = pl.BlockSpec(memory_space=pltpu.VMEM)
    features = back.shape[1]
    return pl.pallas_call(
        functools.partial(combine_kernel, experts, capacity),
        in_specs=[vmem, vmem, pl.BlockSpec(memory_space=pl.ANY)],
        out_specs=(vmem, vmem),
        out_shape=(
            jax.ShapeDtypeStruct((routes.shape[1], features), BF16),
            jax.ShapeDtypeStruct((devices, 8, features // 8), F32),
        ),
        scratch_shapes=[pltpu.VMEM((8, features // 8), F32)],
        compiler_params=pltpu.CompilerParams(vmem_limit_bytes=VMEM_LIMIT),
        name="combine",
    )(routes, back, after)


def run_total(spread, after, experts):
    vmem = pl.BlockSpec(memory_space=pltpu.VMEM)
    devices, chunks, lanes = spread.shape
    return pl.pallas_call(
        total_kernel,
        in_specs=[vmem, pl.BlockSpec(memory_space=pl.ANY)],
        out_specs=vmem,
        out_shape=jax.ShapeDtypeStruct((experts, chunks * lanes), F32),
        compiler_params=pltpu.CompilerParams(vmem_limit_bytes=VMEM_LIMIT),
        name="total",
    )(spread, after)


def run_expert(place, got, router, weights, after=(), tile=256):
    sources, _, stride, features = got.shape
    rows = sources * stride
    hidden = weights[0].shape[1]
    experts = router.shape[0]
    tiles = hidden // tile
    vmem = pl.BlockSpec(memory_space=pltpu.VMEM)
    anywhere = pl.BlockSpec(memory_space=pl.ANY)
    return pl.pallas_call(
        functools.partial(expert_kernel, tile, tiles),
        in_specs=[pl.BlockSpec(memory_space=pltpu.SMEM), vmem]
        + [anywhere] * 3
        + [vmem]
        + [anywhere] * len(after),
        out_specs=vmem,
        out_shape=jax.ShapeDtypeStruct((sources, stride, features), BF16),
        scratch_shapes=[pltpu.VMEM((hidden, features), BF16)] * 3
        + [
            pltpu.VMEM((rows, features), F32),
            pltpu.VMEM((rows, 128), F32),
            pltpu.VMEM((3, rows, tile), F32),
            pltpu.VMEM((3, rows, tile), F32),
            pltpu.SemaphoreType.DMA((3, tiles)),
        ],
        compiler_params=pltpu.CompilerParams(vmem_limit_bytes=VMEM_LIMIT),
        cost_estimate=pl.CostEstimate(
            flops=20 * rows * hidden * features,
            bytes_accessed=6 * hidden * features + 6 * rows * features,
            transcendentals=rows * hidden,
        ),
        name="expert_pass",
    )(place, router, *weights, got, *after)


def pass_kernel(value, after, out):
    pass


def run_after(value, after):
    anywhere = pl.BlockSpec(memory_space=pl.ANY)
    return pl.pallas_call(
        pass_kernel,
        in_specs=[anywhere, anywhere],
        out_specs=anywhere,
        out_shape=jax.ShapeDtypeStruct(value.shape, value.dtype),
        input_output_aliases={0: 0},
        name="after",
    )(value, after)


def run_weight(place, router, weights, pieces, before, slices, after=(), effort=1):
    features = router.shape[1]
    hidden = weights[0].shape[1] // slices
    size, stride = pieces[0].shape[0] // 2, pieces[0].shape[2]
    unit = size * stride
    parts_of = [(i, h) for i, piece in enumerate(pieces) for h in range(piece.shape[0] // size)]
    units = len(parts_of)
    vmem = pl.BlockSpec(memory_space=pltpu.VMEM)
    anywhere = pl.BlockSpec(memory_space=pl.ANY)
    extra = [*after, *([] if before is None else [before])]
    return pl.pallas_call(
        functools.partial(weight_kernel, parts_of, len(pieces), before is None),
        in_specs=[pl.BlockSpec(memory_space=pltpu.SMEM), vmem]
        + [anywhere] * 3
        + [vmem] * len(pieces)
        + [anywhere] * len(extra),
        out_specs=anywhere,
        out_shape=jax.ShapeDtypeStruct((3, hidden, features), BF16),
        scratch_shapes=[
            pltpu.VMEM((3, hidden, features), BF16),
            pltpu.VMEM((3, hidden, unit), F32),
            pltpu.VMEM((3, hidden, unit), F32),
            pltpu.VMEM((3, hidden, units * unit), BF16),
            pltpu.VMEM((3, hidden if before is not None else STRIDE, features), BF16),
            pltpu.VMEM((3, hidden, features), BF16),
            pltpu.SemaphoreType.DMA((3,)),
            pltpu.SemaphoreType.DMA((6,)),
        ],
        compiler_params=pltpu.CompilerParams(vmem_limit_bytes=VMEM_LIMIT),
        cost_estimate=pl.CostEstimate(
            flops=effort * units * unit * hidden * features,
            bytes_accessed=units * unit * features,
            transcendentals=0,
        ),
        name="weight_grads",
    )(place, router, *weights, *pieces, *extra)


def shift(value, axis, step):
    size = lax.axis_size(axis)
    return lax.ppermute(value, axis, [(i, (i + step) % size) for i in range(size)])


def share(value, axes):
    return lax.all_to_all(value, axes, split_axis=0, concat_axis=0, tiled=True)


def shards(tokens, out_grad, routes, router_weight, gate_weight, up_weight, down_weight):
    count_tok, features = tokens.shape
    experts = router_weight.shape[1]
    capacity = 5 * count_tok * 2 // (4 * experts)
    routes_t = routes.T
    router = router_weight.T
    weights = (gate_weight, up_weight, down_weight)
    expert = lax.axis_index("expert").astype(jnp.int32)
    group = lax.axis_index("dp").astype(jnp.int32)
    place = jnp.stack([expert, group])
    slices = lax.axis_size("dp")
    devices = slices * lax.axis_size("expert")

    def send(tokens, out_grad, routes):
        sent = run_dispatch(tokens, out_grad, routes, experts, capacity)
        return sent, share(sent, "expert").reshape(experts, 2, STRIDE, features)

    far_inputs = [shift(v, "dp", 2) for v in (tokens, out_grad, routes_t)]
    _, own = send(tokens, out_grad, routes_t)
    far_sent, far = send(*far_inputs)
    left, right = shift(own, "dp", 1), shift(own, "dp", -1)

    row_grads = run_expert(place, own, router, weights, after=(far_sent,))
    row_grads = run_after(row_grads, far)
    back = share(row_grads, "expert").reshape(-1, features)

    weight = functools.partial(run_weight, place, router, weights, slices=slices)
    early = weight([own, far], None, after=(row_grads,), effort=0)
    grads = weight([left, right], early, effort=20)
    in_grad, spread = run_combine(routes_t, back, early, experts, capacity, devices)
    grad_router = run_total(share(spread, ("expert", "dp")), grads, experts)
    return (in_grad, jnp.transpose(grads, (1, 0, 2))[None], grad_router.T)


def solution(mesh):
    in_specs = (
        P(("expert", "dp"), None),
        P(("expert", "dp"), None),
        P(("expert", "dp"), None),
        P(),
        P("expert", None, None),
        P("expert", None, None),
        P("expert", None, None),
    )
    out_specs = (P(("expert", "dp"), None), P("expert", "dp", None, None), P())
    return jax.shard_map(shards, mesh=mesh, in_specs=in_specs, out_specs=out_specs, check_vma=False)
```

profile of v0, /device:TPU:1, one launch (start us, length us, event | category | flops | bytes accessed | tf_op | source)
XLA Modules:
  0.0 136.4 jit_solution(9366048513870946826)
XLA Ops:
  0.6 3.3 %dispatch.2 = bf16[32,32,1024]{2,1,0:T(8,128)(2,1)} custom-call(bf16[192,1024]{1,0:T(8,128)(2,1)} %tokens.1, bf16[192,1024]{1,0:T(8,128)(2,1)} %out_grad.1, s32[2,192]{1,0:T(2,128)} %bitcast.23), custom_call_target="tpu_custom_call" | custom-call | tf_op jit(solution)/shard_map/dispatch/pallas_call | solution.py:301
  3.9 0.0 copy-start.4
  3.9 0.0 copy-start.5
  3.9 0.0 copy-start.7
  3.9 9.6 %all-to-all-start = ((bf16[32,32,1024]{2,1,0:T(8,128)(2,1)}), bf16[32,32,1024]{2,1,0:T(8,128)(2,1)S(1)}, u32[]{:S(2)}, u32[]{:S(2)}) async-start(bf16[32,32,1024]{2,1,0:T(8,128)(2,1)} %dispatch.2), calls=%async_computation | async-start | bytes 4194304 | tf_op jit(solution)/shard_map/all_to_all | solution.py:433
  13.5 0.0 copy-done.4
  13.5 3.0 %collective-permute-start = (bf16[192,1024]{1,0:T(8,128)(2,1)S(1)}, bf16[192,1024]{1,0:T(8,128)(2,1)S(1)}, u32[]{:S(2)}, u32[]{:S(2)}) collective-permute-start(bf16[192,1024]{1,0:T(8,128)(2,1)S(1)} %copy-done.4), channel_id=1, source_target_pairs={{0,2},{1,3},{2,0},{3,1},{4,6},{5,7},{6,4},{7,5},{8,10},{9,11},{10,... | collective-permute-start | bytes 1179656 | tf_op jit(solution)/shard_map/ppermute | solution.py:429
  16.5 0.0 copy-done.5
  16.5 0.1 collective-permute-start.1
  16.6 0.0 copy-done.7
  16.6 2.9 %collective-permute-start.2 = (s32[2,192]{1,0:T(2,128)S(1)}, s32[2,192]{1,0:T(2,128)S(1)}, u32[]{:S(2)}, u32[]{:S(2)}) collective-permute-start(s32[2,192]{1,0:T(2,128)S(1)} %bitcast.25), channel_id=1, source_target_pairs={{0,2},{1,3},{2,0},{3,1},{4,6},{5,7},{6,4},{7,5},{8,10},{9,11},{10,... | collective-permute-start | bytes 4616 | tf_op jit(solution)/shard_map/ppermute | solution.py:429
  19.5 0.6 pad_add_fusion.refs_0_
  20.1 14.0 %collective-permute-done.2.routes = s32[2,192]{1,0:T(2,128)S(1)} collective-permute-done((s32[2,192]{1,0:T(2,128)S(1)}, s32[2,192]{1,0:T(2,128)S(1)}, u32[]{:S(2)}, u32[]{:S(2)}) %collective-permute-start.2) | collective-permute-done | bytes 1568 | tf_op jit(solution)/shard_map/ppermute | solution.py:429
  34.2 0.0 copy-start.8
  34.2 0.0 collective-permute-done.tokens
  34.2 0.0 copy-start.6
  34.2 0.0 collective-permute-done.1.out_grad
  34.2 0.6 copy-done.8
  34.7 0.2 copy-done.6
  34.9 3.3 %dispatch.3.refs_6_ = bf16[32,32,1024]{2,1,0:T(8,128)(2,1)} custom-call(bf16[192,1024]{1,0:T(8,128)(2,1)} %copy-done.6, bf16[192,1024]{1,0:T(8,128)(2,1)} %collective-permute-done.1.out_grad, s32[2,192]{1,0:T(2,128)} %copy-done.8), custom_call_target="tpu_custom_call" | custom-call | tf_op jit(solution)/shard_map/dispatch/pallas_call | solution.py:301
  38.2 3.1 %all-to-all-done = bf16[32,32,1024]{2,1,0:T(8,128)(2,1)S(1)} async-done(((bf16[32,32,1024]{2,1,0:T(8,128)(2,1)}), bf16[32,32,1024]{2,1,0:T(8,128)(2,1)S(1)}, u32[]{:S(2)}, u32[]{:S(2)}) %all-to-all-start) | async-done | bytes 2097184 | tf_op jit(solution)/shard_map/all_to_all | solution.py:433
  41.3 0.0 copy-start.1
  41.4 1.3 copy-done.1
  42.7 6.0 %all-to-all-start.1 = ((bf16[32,32,1024]{2,1,0:T(8,128)(2,1)}), bf16[32,32,1024]{2,1,0:T(8,128)(2,1)S(1)}, u32[]{:S(2)}, u32[]{:S(2)}) async-start(bf16[32,32,1024]{2,1,0:T(8,128)(2,1)} %dispatch.3.refs_6_), calls=%async_computation.1 | async-start | bytes 4194304 | tf_op jit(solution)/shard_map/all_to_all | solution.py:433
  48.7 1.4 %collective-permute-start.3 = (bf16[32,2,16,1024]{3,2,1,0:T(8,128)(2,1)}, bf16[32,2,16,1024]{3,2,1,0:T(8,128)(2,1)}, u32[]{:S(2)}, u32[]{:S(2)}) collective-permute-start(bf16[32,2,16,1024]{3,2,1,0:T(8,128)(2,1)} %bitcast.13), channel_id=1, source_target_pairs={{0,1},{1,2},{2,3},{3,0},{4,5},{5,6},{6,7},{7,4},{8,9},{9,10},{10,1... | collective-permute-start | bytes 6291464 | tf_op jit(solution)/shard_map/ppermute | solution.py:429
  50.1 1.5 %collective-permute-start.4 = (bf16[32,2,16,1024]{3,2,1,0:T(8,128)(2,1)}, bf16[32,2,16,1024]{3,2,1,0:T(8,128)(2,1)}, u32[]{:S(2)}, u32[]{:S(2)}) collective-permute-start(bf16[32,2,16,1024]{3,2,1,0:T(8,128)(2,1)} %bitcast.14), channel_id=1, source_target_pairs={{0,3},{1,0},{2,1},{3,2},{4,7},{5,4},{6,5},{7,6},{8,11},{9,8},{10,9... | collective-permute-start | bytes 6291464 | tf_op jit(solution)/shard_map/ppermute | solution.py:429
  51.6 24.1 %expert_pass.1.value = bf16[32,16,1024]{2,1,0:T(8,128)(2,1)} custom-call(s32[2]{0:T(128)} %pad_add_fusion.refs_0_, f32[32,1024]{1,0:T(8,128)} %bitcast.19, bf16[1,2816,1024]{2,1,0:T(8,128)(2,1)} %refs_2_.5, bf16[1,2816,1024]{2,1,0:T(8,128)(2,1)} %refs_3_.5, bf16[1,2816,1024]{2,1,0:T(8,128)(2,1)} %refs_4_.5, bf16[32,2,16,1024]{3,2,1,0:T(8,128)(2,1)} %bitcast.15, ...), custom_call_target="tpu_custom_call" | custom-call | flops 29527900160 | bytes 20447232 | tf_op jit(solution)/shard_map/expert_pass/pallas_call | solution.py:347
  75.7 1.0 all-to-all-done.1
  76.7 0.0 copy-start
  76.7 1.4 %copy-done = bf16[32,32,1024]{2,1,0:T(8,128)(2,1)} copy-done((bf16[32,32,1024]{2,1,0:T(8,128)(2,1)}, bf16[32,32,1024]{2,1,0:T(8,128)(2,1)S(1)}, u32[]{:S(2)}) %copy-start) | copy-done | bytes 2097176
  78.1 6.9 %all-to-all-start.2 = ((bf16[32,16,1024]{2,1,0:T(8,128)(2,1)}), bf16[32,16,1024]{2,1,0:T(8,128)(2,1)S(1)}, u32[]{:S(2)}, u32[]{:S(2)}) async-start(bf16[32,16,1024]{2,1,0:T(8,128)(2,1)} %after.1.refs_7_), calls=%async_computation.2 | async-start | bytes 2097152 | tf_op jit(solution)/shard_map/all_to_all | solution.py:433
  85.0 16.5 %weight_grads.2.after.refs_7_ = bf16[3,704,1024]{2,1,0:T(8,128)(2,1)} custom-call(s32[2]{0:T(128)} %pad_add_fusion.refs_0_, f32[32,1024]{1,0:T(8,128)} %bitcast.20, bf16[1,2816,1024]{2,1,0:T(8,128)(2,1)} %refs_2_.5, bf16[1,2816,1024]{2,1,0:T(8,128)(2,1)} %refs_3_.5, bf16[1,2816,1024]{2,1,0:T(8,128)(2,1)} %refs_4_.5, bf16[32,2,16,1024]{3,2,1,0:T(8,128)(2,1)} %bitcast.16, ...), custom_call_target="tpu_custom_call" | custom-call | bytes 1048576 | tf_op jit(solution)/shard_map/weight_grads/pallas_call | solution.py:399
  101.5 0.7 all-to-all-done.2
  102.2 0.0 copy-start.2
  102.2 1.0 copy-done.2
  103.2 2.7 %combine.1 = (bf16[192,1024]{1,0:T(8,128)(2,1)}, f32[128,8,128]{2,1,0:T(8,128)}) custom-call(s32[2,192]{1,0:T(2,128)} %bitcast.24, bf16[512,1024]{1,0:T(8,128)(2,1)} %bitcast.18, bf16[3,704,1024]{2,1,0:T(8,128)(2,1)} %weight_grads.2.after.refs_7_), custom_call_target="tpu_custom_call" | custom-call | tf_op jit(solution)/shard_map/combine/pallas_call | solution.py:312
  105.9 7.9 %all-to-all-start.3 = ((f32[128,8,128]{2,1,0:T(8,128)}), f32[128,8,128]{2,1,0:T(8,128)S(1)}, u32[]{:S(2)}, u32[]{:S(2)}) async-start(f32[128,8,128]{2,1,0:T(8,128)} %get-tuple-element.6), calls=%async_computation.3 | async-start | bytes 1048576 | tf_op jit(solution)/shard_map/all_to_all | solution.py:433
  113.9 0.0 collective-permute-done.3.refs_5_
  113.9 0.0 collective-permute-done.4.refs_6_
  113.9 20.0 %weight_grads.3.after = bf16[3,704,1024]{2,1,0:T(8,128)(2,1)} custom-call(s32[2]{0:T(128)} %pad_add_fusion.refs_0_, f32[32,1024]{1,0:T(8,128)} %bitcast.21, bf16[1,2816,1024]{2,1,0:T(8,128)(2,1)} %refs_2_.5, bf16[1,2816,1024]{2,1,0:T(8,128)(2,1)} %refs_3_.5, bf16[1,2816,1024]{2,1,0:T(8,128)(2,1)} %refs_4_.5, ...), custom_call_target="tpu_custom_call" | custom-call | flops 14763950080 | bytes 1048576 | tf_op jit(solution)/shard_map/weight_grads/pallas_call | solution.py:399
  133.8 0.0 all-to-all-done.3.spread
  133.9 0.0 copy-start.3
  133.9 0.8 copy-done.3
  134.7 1.8 %total.1 = f32[32,1024]{1,0:T(8,128)} custom-call(f32[128,8,128]{2,1,0:T(8,128)} %copy-done.3, bf16[3,704,1024]{2,1,0:T(8,128)(2,1)} %weight_grads.3.after), custom_call_target="tpu_custom_call" | custom-call | tf_op jit(solution)/shard_map/total/pallas_call | solution.py:329
  (1 shorter events, 0.0 us)
Async XLA Ops:
  3.9 9.6 %copy-start.4 = (bf16[192,1024]{1,0:T(8,128)(2,1)S(1)}, bf16[192,1024]{1,0:T(8,128)(2,1)}, u32[]{:S(2)}) copy-start(bf16[192,1024]{1,0:T(8,128)(2,1)} %tokens.1) | copy-start | bytes 1179652
  3.9 12.6 %copy-start.5 = (bf16[192,1024]{1,0:T(8,128)(2,1)S(1)}, bf16[192,1024]{1,0:T(8,128)(2,1)}, u32[]{:S(2)}) copy-start(bf16[192,1024]{1,0:T(8,128)(2,1)} %out_grad.1) | copy-start | bytes 1179652
  3.9 12.7 %copy-start.7 = (s32[192,2]{0,1:T(2,128)S(1)}, s32[192,2]{0,1:T(2,128)}, u32[]{:S(2)}) copy-start(s32[192,2]{0,1:T(2,128)} %param.9) | copy-start | bytes 4612
  3.9 37.4 %all-to-all-start = ((bf16[32,32,1024]{2,1,0:T(8,128)(2,1)}), bf16[32,32,1024]{2,1,0:T(8,128)(2,1)S(1)}, u32[]{:S(2)}, u32[]{:S(2)}) async-start(bf16[32,32,1024]{2,1,0:T(8,128)(2,1)} %dispatch.2), calls=%async_computation | async-start | bytes 4194304 | tf_op jit(solution)/shard_map/all_to_all | solution.py:433
  13.5 20.6 %collective-permute-start = (bf16[192,1024]{1,0:T(8,128)(2,1)S(1)}, bf16[192,1024]{1,0:T(8,128)(2,1)S(1)}, u32[]{:S(2)}, u32[]{:S(2)}) collective-permute-start(bf16[192,1024]{1,0:T(8,128)(2,1)S(1)} %copy-done.4), channel_id=1, source_target_pairs={{0,2},{1,3},{2,0},{3,1},{4,6},{5,7},{6,4},{7,5},{8,10},{9,11},{10,... | collective-permute-start | bytes 1179656 | tf_op jit(solution)/shard_map/ppermute | solution.py:429
  16.5 17.6 %collective-permute-start.1 = (bf16[192,1024]{1,0:T(8,128)(2,1)S(1)}, bf16[192,1024]{1,0:T(8,128)(2,1)}, u32[]{:S(2)}, u32[]{:S(2)}) collective-permute-start(bf16[192,1024]{1,0:T(8,128)(2,1)S(1)} %copy-done.5), channel_id=1, source_target_pairs={{0,2},{1,3},{2,0},{3,1},{4,6},{5,7},{6,4},{7,5},{8,10},{9,11},{10,... | collective-permute-start | bytes 1179656 | tf_op jit(solution)/shard_map/ppermute | solution.py:429
  16.6 17.5 %collective-permute-start.2 = (s32[2,192]{1,0:T(2,128)S(1)}, s32[2,192]{1,0:T(2,128)S(1)}, u32[]{:S(2)}, u32[]{:S(2)}) collective-permute-start(s32[2,192]{1,0:T(2,128)S(1)} %bitcast.25), channel_id=1, source_target_pairs={{0,2},{1,3},{2,0},{3,1},{4,6},{5,7},{6,4},{7,5},{8,10},{9,11},{10,... | collective-permute-start | bytes 4616 | tf_op jit(solution)/shard_map/ppermute | solution.py:429
  34.2 0.6 copy-start.8
  34.2 0.7 copy-start.6
  41.3 1.3 copy-start.1
  42.7 34.0 %all-to-all-start.1 = ((bf16[32,32,1024]{2,1,0:T(8,128)(2,1)}), bf16[32,32,1024]{2,1,0:T(8,128)(2,1)S(1)}, u32[]{:S(2)}, u32[]{:S(2)}) async-start(bf16[32,32,1024]{2,1,0:T(8,128)(2,1)} %dispatch.3.refs_6_), calls=%async_computation.1 | async-start | bytes 4194304 | tf_op jit(solution)/shard_map/all_to_all | solution.py:433
  48.7 65.1 %collective-permute-start.3 = (bf16[32,2,16,1024]{3,2,1,0:T(8,128)(2,1)}, bf16[32,2,16,1024]{3,2,1,0:T(8,128)(2,1)}, u32[]{:S(2)}, u32[]{:S(2)}) collective-permute-start(bf16[32,2,16,1024]{3,2,1,0:T(8,128)(2,1)} %bitcast.13), channel_id=1, source_target_pairs={{0,1},{1,2},{2,3},{3,0},{4,5},{5,6},{6,7},{7,4},{8,9},{9,10},{10,1... | collective-permute-start | bytes 6291464 | tf_op jit(solution)/shard_map/ppermute | solution.py:429
  50.1 63.8 %collective-permute-start.4 = (bf16[32,2,16,1024]{3,2,1,0:T(8,128)(2,1)}, bf16[32,2,16,1024]{3,2,1,0:T(8,128)(2,1)}, u32[]{:S(2)}, u32[]{:S(2)}) collective-permute-start(bf16[32,2,16,1024]{3,2,1,0:T(8,128)(2,1)} %bitcast.14), channel_id=1, source_target_pairs={{0,3},{1,0},{2,1},{3,2},{4,7},{5,4},{6,5},{7,6},{8,11},{9,8},{10,9... | collective-permute-start | bytes 6291464 | tf_op jit(solution)/shard_map/ppermute | solution.py:429
  76.7 1.4 %copy-start = (bf16[32,32,1024]{2,1,0:T(8,128)(2,1)}, bf16[32,32,1024]{2,1,0:T(8,128)(2,1)S(1)}, u32[]{:S(2)}) copy-start(bf16[32,32,1024]{2,1,0:T(8,128)(2,1)S(1)} %all-to-all-done.1) | copy-start | bytes 6291460
  78.1 24.1 %all-to-all-start.2 = ((bf16[32,16,1024]{2,1,0:T(8,128)(2,1)}), bf16[32,16,1024]{2,1,0:T(8,128)(2,1)S(1)}, u32[]{:S(2)}, u32[]{:S(2)}) async-start(bf16[32,16,1024]{2,1,0:T(8,128)(2,1)} %after.1.refs_7_), calls=%async_computation.2 | async-start | bytes 2097152 | tf_op jit(solution)/shard_map/all_to_all | solution.py:433
  102.2 1.0 copy-start.2
  105.9 27.9 %all-to-all-start.3 = ((f32[128,8,128]{2,1,0:T(8,128)}), f32[128,8,128]{2,1,0:T(8,128)S(1)}, u32[]{:S(2)}, u32[]{:S(2)}) async-start(f32[128,8,128]{2,1,0:T(8,128)} %get-tuple-element.6), calls=%async_computation.3 | async-start | bytes 1048576 | tf_op jit(solution)/shard_map/all_to_all | solution.py:433
  133.9 0.8 copy-start.3
where the time goes:
time: 137 us; the launch traced here: 136 us
  Pallas kernels  71.6 us (52%)
  starting transfers between devices  39.3 us (29%)
  waiting for transfers between devices  18.9 us (14%)
  local copies, waits for them, and re-layouts  5.29 us (4%)
    pallas_call x2, Pallas kernels, run_weight(): pl.pallas_call(functools.partial(weight_kernel, parts_of, len(pieces), be...  36.4 us
    all_to_all x4, starting transfers between devices, share(): return lax.all_to_all(value, axes, split_axis=0, concat_axis=0, tiled=True)  30.5 us
    pallas_call x1, Pallas kernels, run_expert(): pl.pallas_call(functools.partial(expert_kernel, tile, tiles), in_specs=[p...  24.1 us
    ppermute x5, waiting for transfers between devices, shift(): lax.ppermute(value, axis, [(i, (i + step) % size) for i in range(size)])  14 us
    ppermute x5, starting transfers between devices, shift(): lax.ppermute(value, axis, [(i, (i + step) % size) for i in range(size)])  8.87 us
    pallas_call x2, Pallas kernels, run_dispatch(): pl.pallas_call(functools.partial(dispatch_kernel, experts, capacity), out...  6.61 us
    unnamed x18, local copies, waits for them, and re-layouts  5.29 us
    all_to_all x4, waiting for transfers between devices, share(): return lax.all_to_all(value, axes, split_axis=0, concat_axis=0, tiled=True)  4.83 us
  transfers between devices with their start and end apart: 9, of which 4 were waited for; matrix products, arithmetic and copies ran while one was open for 0% of the time, Pallas kernels for 49%

commit v1 on v0

--- a/solution.py
+++ b/solution.py
@@ -11,7 +11,7 @@
 STRIDE = 16
 F32 = jnp.float32
 BF16 = jnp.bfloat16
-VMEM_LIMIT = 60 * 1024 * 1024
+VMEM_LIMIT = 64 * 1024 * 1024
 
 FEATURE_DIMS = (((1,), (1,)), ((), ()))
 ROW_DIMS = (((0,), (0,)), ((), ()))
@@ -278,6 +278,9 @@
         if u + 1 < units:
             prepare(u + 1, slots[(u + 1) % 2])
         finish(u, slots[u % 2])
+    if not first:
+        for k in range(3):
+            before_copy(k).wait()
     for k in range(3):
         value = None
         for i, source in enumerate(sources):
@@ -288,7 +291,6 @@
             )
             value = part if value is None else value + part
         if not first:
-            before_copy(k).wait()
             value = value + total[k].astype(F32)
         stage[k] = value.astype(stage.dtype)
         out_copy(k).start()

time: 137 us -> 132 us (0.964)
  local copies, waits for them, and re-layouts: 5.29 us -> 1.33 us
  Pallas kernels: 71.6 us -> 68.8 us
  starting transfers between devices: 39.3 us -> 41.2 us
    unnamed x18 -> x10, local copies, waits for them, and re-layouts: 5.29 us -> 1.33 us
    pallas_call x2, Pallas kernels: 36.4 us -> 33.7 us  [run_weight(): pl.pallas_call(functools.partial(weight_kernel, parts_of, len(pieces), be...]
    all_to_all x4, starting transfers between devices: 30.5 us -> 32.3 us  [share(): return lax.all_to_all(value, axes, split_axis=0, concat_axis=0, tiled=True)]
where the time goes in v1:
time: 132 us; the launch traced here: 131 us
  Pallas kernels  68.8 us (52%)
  starting transfers between devices  41.2 us (31%)
  waiting for transfers between devices  18.4 us (14%)
  local copies, waits for them, and re-layouts  1.33 us (1%)
    pallas_call x2, Pallas kernels, run_weight(): pl.pallas_call(functools.partial(weight_kernel, parts_of, len(pieces), be...  33.7 us
    all_to_all x4, starting transfers between devices, share(): return lax.all_to_all(value, axes, split_axis=0, concat_axis=0, tiled=True)  32.3 us
    pallas_call x1, Pallas kernels, run_expert(): pl.pallas_call(functools.partial(expert_kernel, tile, tiles), in_specs=[p...  24 us
    ppermute x5, waiting for transfers between devices, shift(): lax.ppermute(value, axis, [(i, (i + step) % size) for i in range(size)])  14 us
    ppermute x5, starting transfers between devices, shift(): lax.ppermute(value, axis, [(i, (i + step) % size) for i in range(size)])  8.87 us
    pallas_call x2, Pallas kernels, run_dispatch(): pl.pallas_call(functools.partial(dispatch_kernel, experts, capacity), out...  6.62 us
    all_to_all x4, waiting for transfers between devices, share(): return lax.all_to_all(value, axes, split_axis=0, concat_axis=0, tiled=True)  4.46 us
    pallas_call x1, Pallas kernels, run_combine(): pl.pallas_call(functools.partial(combine_kernel, experts, capacity), in_s...  2.72 us
  transfers between devices with their start and end apart: 9, of which 4 were waited for; matrix products, arithmetic and copies ran while one was open for 0% of the time, Pallas kernels for 49%

profile of v1, /device:TPU:1, one launch (start us, length us, event | category | flops | bytes accessed | tf_op | source)
XLA Modules:
  0.0 131.1 jit_solution(14797397894123908647)
XLA Ops:
  0.6 3.3 %dispatch.2 = bf16[32,32,1024]{2,1,0:T(8,128)(2,1)} custom-call(bf16[192,1024]{1,0:T(8,128)(2,1)} %tokens.1, bf16[192,1024]{1,0:T(8,128)(2,1)} %out_grad.1, s32[2,192]{1,0:T(2,128)} %bitcast.16), custom_call_target="tpu_custom_call" | custom-call | tf_op jit(solution)/shard_map/dispatch/pallas_call | solution.py:303
  3.9 0.0 copy-start
  3.9 0.0 copy-start.1
  3.9 0.0 copy-start.3
  3.9 9.6 %all-to-all-start = ((bf16[32,32,1024]{2,1,0:T(8,128)(2,1)}), bf16[32,32,1024]{2,1,0:T(8,128)(2,1)}, u32[]{:S(2)}, u32[]{:S(2)}) async-start(bf16[32,32,1024]{2,1,0:T(8,128)(2,1)} %dispatch.2), calls=%async_computation | async-start | bytes 4194304 | tf_op jit(solution)/shard_map/all_to_all | solution.py:435
  13.6 0.0 copy-done
  13.6 3.0 %collective-permute-start = (bf16[192,1024]{1,0:T(8,128)(2,1)S(1)}, bf16[192,1024]{1,0:T(8,128)(2,1)S(1)}, u32[]{:S(2)}, u32[]{:S(2)}) collective-permute-start(bf16[192,1024]{1,0:T(8,128)(2,1)S(1)} %copy-done), channel_id=1, source_target_pairs={{0,2},{1,3},{2,0},{3,1},{4,6},{5,7},{6,4},{7,5},{8,10},{9,11},{10,... | collective-permute-start | bytes 1179656 | tf_op jit(solution)/shard_map/ppermute | solution.py:431
  16.6 0.0 copy-done.1
  16.6 0.1 collective-permute-start.1
  16.7 0.0 copy-done.3
  16.7 2.9 %collective-permute-start.2 = (s32[2,192]{1,0:T(2,128)S(1)}, s32[2,192]{1,0:T(2,128)S(1)}, u32[]{:S(2)}, u32[]{:S(2)}) collective-permute-start(s32[2,192]{1,0:T(2,128)S(1)} %bitcast.18), channel_id=1, source_target_pairs={{0,2},{1,3},{2,0},{3,1},{4,6},{5,7},{6,4},{7,5},{8,10},{9,11},{10,... | collective-permute-start | bytes 4616 | tf_op jit(solution)/shard_map/ppermute | solution.py:431
  19.5 0.6 pad_add_fusion.refs_0_
  20.2 14.0 %collective-permute-done.2.routes = s32[2,192]{1,0:T(2,128)S(1)} collective-permute-done((s32[2,192]{1,0:T(2,128)S(1)}, s32[2,192]{1,0:T(2,128)S(1)}, u32[]{:S(2)}, u32[]{:S(2)}) %collective-permute-start.2) | collective-permute-done | bytes 1568 | tf_op jit(solution)/shard_map/ppermute | solution.py:431
  34.1 0.0 copy-start.4
  34.1 0.0 collective-permute-done.tokens
  34.1 0.6 copy-done.4
  34.7 0.0 copy-start.2
  34.7 0.7 copy-done.2
  35.4 0.0 collective-permute-done.1.out_grad
  35.5 3.3 %dispatch.3.refs_6_ = bf16[32,32,1024]{2,1,0:T(8,128)(2,1)} custom-call(bf16[192,1024]{1,0:T(8,128)(2,1)} %copy-done.2, bf16[192,1024]{1,0:T(8,128)(2,1)} %collective-permute-done.1.out_grad, s32[2,192]{1,0:T(2,128)} %copy-done.4), custom_call_target="tpu_custom_call" | custom-call | tf_op jit(solution)/shard_map/dispatch/pallas_call | solution.py:303
  38.8 2.7 %all-to-all-done = bf16[32,32,1024]{2,1,0:T(8,128)(2,1)} async-done(((bf16[32,32,1024]{2,1,0:T(8,128)(2,1)}), bf16[32,32,1024]{2,1,0:T(8,128)(2,1)}, u32[]{:S(2)}, u32[]{:S(2)}) %all-to-all-start) | async-done | bytes 2097184 | tf_op jit(solution)/shard_map/all_to_all | solution.py:435
  41.4 6.7 %all-to-all-start.1 = ((bf16[32,32,1024]{2,1,0:T(8,128)(2,1)}), bf16[32,32,1024]{2,1,0:T(8,128)(2,1)}, u32[]{:S(2)}, u32[]{:S(2)}) async-start(bf16[32,32,1024]{2,1,0:T(8,128)(2,1)} %dispatch.3.refs_6_), calls=%async_computation.1 | async-start | bytes 4194304 | tf_op jit(solution)/shard_map/all_to_all | solution.py:435
  48.2 1.4 %collective-permute-start.3 = (bf16[32,2,16,1024]{3,2,1,0:T(8,128)(2,1)}, bf16[32,2,16,1024]{3,2,1,0:T(8,128)(2,1)}, u32[]{:S(2)}, u32[]{:S(2)}) collective-permute-start(bf16[32,2,16,1024]{3,2,1,0:T(8,128)(2,1)} %bitcast.4.refs_5_), channel_id=1, source_target_pairs={{0,1},{1,2},{2,3},{3,0},{4,5},{5,6},{6,7},{7,4},{8,9},{9,10},{10,1... | collective-permute-start | bytes 6291464 | tf_op jit(solution)/shard_map/ppermute | solution.py:431
  49.6 1.5 %collective-permute-start.4 = (bf16[32,2,16,1024]{3,2,1,0:T(8,128)(2,1)}, bf16[32,2,16,1024]{3,2,1,0:T(8,128)(2,1)}, u32[]{:S(2)}, u32[]{:S(2)}) collective-permute-start(bf16[32,2,16,1024]{3,2,1,0:T(8,128)(2,1)} %bitcast.4.refs_5_), channel_id=1, source_target_pairs={{0,3},{1,0},{2,1},{3,2},{4,7},{5,4},{6,5},{7,6},{8,11},{9,8},{10,9... | collective-permute-start | bytes 6291464 | tf_op jit(solution)/shard_map/ppermute | solution.py:431
  51.1 24.0 %expert_pass.1.value = bf16[32,16,1024]{2,1,0:T(8,128)(2,1)} custom-call(s32[2]{0:T(128)} %pad_add_fusion.refs_0_, f32[32,1024]{1,0:T(8,128)} %bitcast.12, bf16[1,2816,1024]{2,1,0:T(8,128)(2,1)} %refs_2_.5, bf16[1,2816,1024]{2,1,0:T(8,128)(2,1)} %refs_3_.5, bf16[1,2816,1024]{2,1,0:T(8,128)(2,1)} %refs_4_.5, bf16[32,2,16,1024]{3,2,1,0:T(8,128)(2,1)} %bitcast.4.refs_5_, ...), custom_call_target="tpu_custom_call" | custom-call | flops 29527900160 | bytes 20447232 | tf_op jit(solution)/shard_map/expert_pass/pallas_call | solution.py:349
  75.1 1.0 all-to-all-done.1
  76.2 7.0 %all-to-all-start.2 = ((bf16[32,16,1024]{2,1,0:T(8,128)(2,1)}), bf16[32,16,1024]{2,1,0:T(8,128)(2,1)}, u32[]{:S(2)}, u32[]{:S(2)}) async-start(bf16[32,16,1024]{2,1,0:T(8,128)(2,1)} %after.1.refs_7_), calls=%async_computation.2 | async-start | bytes 2097152 | tf_op jit(solution)/shard_map/all_to_all | solution.py:435
  83.2 16.5 %weight_grads.2.after.refs_7_ = bf16[3,704,1024]{2,1,0:T(8,128)(2,1)} custom-call(s32[2]{0:T(128)} %pad_add_fusion.refs_0_, f32[32,1024]{1,0:T(8,128)} %bitcast.13, bf16[1,2816,1024]{2,1,0:T(8,128)(2,1)} %refs_2_.5, bf16[1,2816,1024]{2,1,0:T(8,128)(2,1)} %refs_3_.5, bf16[1,2816,1024]{2,1,0:T(8,128)(2,1)} %refs_4_.5, ...), custom_call_target="tpu_custom_call" | custom-call | bytes 1048576 | tf_op jit(solution)/shard_map/weight_grads/pallas_call | solution.py:401
  99.6 0.7 all-to-all-done.2
  100.4 2.7 %combine.1 = (bf16[192,1024]{1,0:T(8,128)(2,1)}, f32[128,8,128]{2,1,0:T(8,128)}) custom-call(s32[2,192]{1,0:T(2,128)} %bitcast.17, bf16[512,1024]{1,0:T(8,128)(2,1)} %bitcast.6.back, bf16[3,704,1024]{2,1,0:T(8,128)(2,1)} %weight_grads.2.after.refs_7_), custom_call_target="tpu_custom_call" | custom-call | tf_op jit(solution)/shard_map/combine/pallas_call | solution.py:314
  103.1 9.0 %all-to-all-start.3 = ((f32[128,8,128]{2,1,0:T(8,128)}), f32[128,8,128]{2,1,0:T(8,128)}, u32[]{:S(2)}, u32[]{:S(2)}) async-start(f32[128,8,128]{2,1,0:T(8,128)} %get-tuple-element.6), calls=%async_computation.3 | async-start | bytes 1048576 | tf_op jit(solution)/shard_map/all_to_all | solution.py:435
  112.1 0.0 collective-permute-done.3.refs_5_
  112.1 0.0 collective-permute-done.4.refs_6_
  112.1 17.2 %weight_grads.3.after = bf16[3,704,1024]{2,1,0:T(8,128)(2,1)} custom-call(s32[2]{0:T(128)} %pad_add_fusion.refs_0_, f32[32,1024]{1,0:T(8,128)} %bitcast.14, bf16[1,2816,1024]{2,1,0:T(8,128)(2,1)} %refs_2_.5, bf16[1,2816,1024]{2,1,0:T(8,128)(2,1)} %refs_3_.5, bf16[1,2816,1024]{2,1,0:T(8,128)(2,1)} %refs_4_.5, ...), custom_call_target="tpu_custom_call" | custom-call | flops 14763950080 | bytes 1048576 | tf_op jit(solution)/shard_map/weight_grads/pallas_call | solution.py:401
  129.3 0.0 all-to-all-done.3.spread
  129.3 1.8 %total.1 = f32[32,1024]{1,0:T(8,128)} custom-call(f32[128,8,128]{2,1,0:T(8,128)} %all-to-all-done.3.spread, bf16[3,704,1024]{2,1,0:T(8,128)(2,1)} %weight_grads.3.after), custom_call_target="tpu_custom_call" | custom-call | tf_op jit(solution)/shard_map/total/pallas_call | solution.py:331
  (1 shorter events, 0.0 us)
Async XLA Ops:
  3.9 9.6 %copy-start = (bf16[192,1024]{1,0:T(8,128)(2,1)S(1)}, bf16[192,1024]{1,0:T(8,128)(2,1)}, u32[]{:S(2)}) copy-start(bf16[192,1024]{1,0:T(8,128)(2,1)} %tokens.1) | copy-start | bytes 1179652
  3.9 12.6 %copy-start.1 = (bf16[192,1024]{1,0:T(8,128)(2,1)S(1)}, bf16[192,1024]{1,0:T(8,128)(2,1)}, u32[]{:S(2)}) copy-start(bf16[192,1024]{1,0:T(8,128)(2,1)} %out_grad.1) | copy-start | bytes 1179652
  3.9 12.7 %copy-start.3 = (s32[192,2]{0,1:T(2,128)S(1)}, s32[192,2]{0,1:T(2,128)}, u32[]{:S(2)}) copy-start(s32[192,2]{0,1:T(2,128)} %param.9) | copy-start | bytes 4612
  3.9 37.5 %all-to-all-start = ((bf16[32,32,1024]{2,1,0:T(8,128)(2,1)}), bf16[32,32,1024]{2,1,0:T(8,128)(2,1)}, u32[]{:S(2)}, u32[]{:S(2)}) async-start(bf16[32,32,1024]{2,1,0:T(8,128)(2,1)} %dispatch.2), calls=%async_computation | async-start | bytes 4194304 | tf_op jit(solution)/shard_map/all_to_all | solution.py:435
  13.6 20.6 %collective-permute-start = (bf16[192,1024]{1,0:T(8,128)(2,1)S(1)}, bf16[192,1024]{1,0:T(8,128)(2,1)S(1)}, u32[]{:S(2)}, u32[]{:S(2)}) collective-permute-start(bf16[192,1024]{1,0:T(8,128)(2,1)S(1)} %copy-done), channel_id=1, source_target_pairs={{0,2},{1,3},{2,0},{3,1},{4,6},{5,7},{6,4},{7,5},{8,10},{9,11},{10,... | collective-permute-start | bytes 1179656 | tf_op jit(solution)/shard_map/ppermute | solution.py:431
  16.6 18.9 %collective-permute-start.1 = (bf16[192,1024]{1,0:T(8,128)(2,1)S(1)}, bf16[192,1024]{1,0:T(8,128)(2,1)}, u32[]{:S(2)}, u32[]{:S(2)}) collective-permute-start(bf16[192,1024]{1,0:T(8,128)(2,1)S(1)} %copy-done.1), channel_id=1, source_target_pairs={{0,2},{1,3},{2,0},{3,1},{4,6},{5,7},{6,4},{7,5},{8,10},{9,11},{10,... | collective-permute-start | bytes 1179656 | tf_op jit(solution)/shard_map/ppermute | solution.py:431
  16.7 17.4 %collective-permute-start.2 = (s32[2,192]{1,0:T(2,128)S(1)}, s32[2,192]{1,0:T(2,128)S(1)}, u32[]{:S(2)}, u32[]{:S(2)}) collective-permute-start(s32[2,192]{1,0:T(2,128)S(1)} %bitcast.18), channel_id=1, source_target_pairs={{0,2},{1,3},{2,0},{3,1},{4,6},{5,7},{6,4},{7,5},{8,10},{9,11},{10,... | collective-permute-start | bytes 4616 | tf_op jit(solution)/shard_map/ppermute | solution.py:431
  34.1 0.6 copy-start.4
  34.7 0.7 copy-start.2
  41.4 34.7 %all-to-all-start.1 = ((bf16[32,32,1024]{2,1,0:T(8,128)(2,1)}), bf16[32,32,1024]{2,1,0:T(8,128)(2,1)}, u32[]{:S(2)}, u32[]{:S(2)}) async-start(bf16[32,32,1024]{2,1,0:T(8,128)(2,1)} %dispatch.3.refs_6_), calls=%async_computation.1 | async-start | bytes 4194304 | tf_op jit(solution)/shard_map/all_to_all | solution.py:435
  48.2 63.9 %collective-permute-start.3 = (bf16[32,2,16,1024]{3,2,1,0:T(8,128)(2,1)}, bf16[32,2,16,1024]{3,2,1,0:T(8,128)(2,1)}, u32[]{:S(2)}, u32[]{:S(2)}) collective-permute-start(bf16[32,2,16,1024]{3,2,1,0:T(8,128)(2,1)} %bitcast.4.refs_5_), channel_id=1, source_target_pairs={{0,1},{1,2},{2,3},{3,0},{4,5},{5,6},{6,7},{7,4},{8,9},{9,10},{10,1... | collective-permute-start | bytes 6291464 | tf_op jit(solution)/shard_map/ppermute | solution.py:431
  49.6 62.5 %collective-permute-start.4 = (bf16[32,2,16,1024]{3,2,1,0:T(8,128)(2,1)}, bf16[32,2,16,1024]{3,2,1,0:T(8,128)(2,1)}, u32[]{:S(2)}, u32[]{:S(2)}) collective-permute-start(bf16[32,2,16,1024]{3,2,1,0:T(8,128)(2,1)} %bitcast.4.refs_5_), channel_id=1, source_target_pairs={{0,3},{1,0},{2,1},{3,2},{4,7},{5,4},{6,5},{7,6},{8,11},{9,8},{10,9... | collective-permute-start | bytes 6291464 | tf_op jit(solution)/shard_map/ppermute | solution.py:431
  76.2 24.2 %all-to-all-start.2 = ((bf16[32,16,1024]{2,1,0:T(8,128)(2,1)}), bf16[32,16,1024]{2,1,0:T(8,128)(2,1)}, u32[]{:S(2)}, u32[]{:S(2)}) async-start(bf16[32,16,1024]{2,1,0:T(8,128)(2,1)} %after.1.refs_7_), calls=%async_computation.2 | async-start | bytes 2097152 | tf_op jit(solution)/shard_map/all_to_all | solution.py:435
  103.1 26.2 %all-to-all-start.3 = ((f32[128,8,128]{2,1,0:T(8,128)}), f32[128,8,128]{2,1,0:T(8,128)}, u32[]{:S(2)}, u32[]{:S(2)}) async-start(f32[128,8,128]{2,1,0:T(8,128)} %get-tuple-element.6), calls=%async_computation.3 | async-start | bytes 1048576 | tf_op jit(solution)/shard_map/all_to_all | solution.py:435

commit v2 on v1

--- a/solution.py
+++ b/solution.py
@@ -225,7 +225,7 @@
 
     def rows(k, u):
         source, part = parts_of[u]
-        size = sources[source].shape[0] // 2
+        size = sources[source].shape[0]
         return sources[source][part * size : (part + 1) * size, k].reshape(unit, features)
 
     def rows_x(u):
@@ -284,7 +284,7 @@
     for k in range(3):
         value = None
         for i, source in enumerate(sources):
-            count_rows = 2 * unit
+            count_rows = unit
             part = dot(
                 terms[k, :, i * count_rows : (i + 1) * count_rows],
                 source[:, k // 2].reshape(count_rows, features),
@@ -391,7 +391,7 @@
 def run_weight(place, router, weights, pieces, before, slices, after=(), effort=1):
     features = router.shape[1]
     hidden = weights[0].shape[1] // slices
-    size, stride = pieces[0].shape[0] // 2, pieces[0].shape[2]
+    size, stride = pieces[0].shape[0], pieces[0].shape[2]
     unit = size * stride
     parts_of = [(i, h) for i, piece in enumerate(pieces) for h in range(piece.shape[0] // size)]
     units = len(parts_of)

time: 132 us -> 130 us (0.985)
  Pallas kernels: 68.8 us -> 66.9 us
    pallas_call x2, Pallas kernels: 33.7 us -> 31.7 us  [run_weight(): pl.pallas_call(functools.partial(weight_kernel, parts_of, len(pieces), be...]
  transfers between devices with their start and end apart: 9 -> 9, of which waited for: 4 -> 4; matrix products, arithmetic and copies ran while one was open for 0% -> 0% of each run, Pallas kernels for 49% -> 48%
where the time goes in v2:
time: 130 us; the launch traced here: 129 us
  Pallas kernels  66.9 us (51%)
  starting transfers between devices  40.3 us (31%)
  waiting for transfers between devices  19.4 us (15%)
  local copies, waits for them, and re-layouts  1.33 us (1%)
    pallas_call x2, Pallas kernels, run_weight(): pl.pallas_call(functools.partial(weight_kernel, parts_of, len(pieces), be...  31.7 us
    all_to_all x4, starting transfers between devices, share(): return lax.all_to_all(value, axes, split_axis=0, concat_axis=0, tiled=True)  31.4 us
    pallas_call x1, Pallas kernels, run_expert(): pl.pallas_call(functools.partial(expert_kernel, tile, tiles), in_specs=[p...  24 us
    ppermute x5, waiting for transfers between devices, shift(): lax.ppermute(value, axis, [(i, (i + step) % size) for i in range(size)])  14 us
    ppermute x5, starting transfers between devices, shift(): lax.ppermute(value, axis, [(i, (i + step) % size) for i in range(size)])  8.87 us
    pallas_call x2, Pallas kernels, run_dispatch(): pl.pallas_call(functools.partial(dispatch_kernel, experts, capacity), out...  6.62 us
    all_to_all x4, waiting for transfers between devices, share(): return lax.all_to_all(value, axes, split_axis=0, concat_axis=0, tiled=True)  5.38 us
    pallas_call x1, Pallas kernels, run_combine(): pl.pallas_call(functools.partial(combine_kernel, experts, capacity), in_s...  2.72 us
  transfers between devices with their start and end apart: 9, of which 4 were waited for; matrix products, arithmetic and copies ran while one was open for 0% of the time, Pallas kernels for 48%

profile of v2, /device:TPU:1, one launch (start us, length us, event | category | flops | bytes accessed | tf_op | source)
XLA Modules:
  0.0 129.2 jit_solution(12718633501385521834)
XLA Ops:
  0.6 3.3 %dispatch.2 = bf16[32,32,1024]{2,1,0:T(8,128)(2,1)} custom-call(bf16[192,1024]{1,0:T(8,128)(2,1)} %tokens.1, bf16[192,1024]{1,0:T(8,128)(2,1)} %out_grad.1, s32[2,192]{1,0:T(2,128)} %bitcast.16), custom_call_target="tpu_custom_call" | custom-call | tf_op jit(solution)/shard_map/dispatch/pallas_call | solution.py:303
  3.9 0.0 copy-start
  3.9 0.0 copy-start.1
  3.9 0.0 copy-start.3
  3.9 9.6 %all-to-all-start = ((bf16[32,32,1024]{2,1,0:T(8,128)(2,1)}), bf16[32,32,1024]{2,1,0:T(8,128)(2,1)}, u32[]{:S(2)}, u32[]{:S(2)}) async-start(bf16[32,32,1024]{2,1,0:T(8,128)(2,1)} %dispatch.2), calls=%async_computation | async-start | bytes 4194304 | tf_op jit(solution)/shard_map/all_to_all | solution.py:435
  13.6 0.0 copy-done
  13.6 3.0 %collective-permute-start = (bf16[192,1024]{1,0:T(8,128)(2,1)S(1)}, bf16[192,1024]{1,0:T(8,128)(2,1)S(1)}, u32[]{:S(2)}, u32[]{:S(2)}) collective-permute-start(bf16[192,1024]{1,0:T(8,128)(2,1)S(1)} %copy-done), channel_id=1, source_target_pairs={{0,2},{1,3},{2,0},{3,1},{4,6},{5,7},{6,4},{7,5},{8,10},{9,11},{10,... | collective-permute-start | bytes 1179656 | tf_op jit(solution)/shard_map/ppermute | solution.py:431
  16.6 0.0 copy-done.1
  16.6 0.1 collective-permute-start.1
  16.7 0.0 copy-done.3
  16.7 2.9 %collective-permute-start.2 = (s32[2,192]{1,0:T(2,128)S(1)}, s32[2,192]{1,0:T(2,128)S(1)}, u32[]{:S(2)}, u32[]{:S(2)}) collective-permute-start(s32[2,192]{1,0:T(2,128)S(1)} %bitcast.18), channel_id=1, source_target_pairs={{0,2},{1,3},{2,0},{3,1},{4,6},{5,7},{6,4},{7,5},{8,10},{9,11},{10,... | collective-permute-start | bytes 4616 | tf_op jit(solution)/shard_map/ppermute | solution.py:431
  19.5 0.6 pad_add_fusion.refs_0_
  20.2 14.0 %collective-permute-done.2.routes = s32[2,192]{1,0:T(2,128)S(1)} collective-permute-done((s32[2,192]{1,0:T(2,128)S(1)}, s32[2,192]{1,0:T(2,128)S(1)}, u32[]{:S(2)}, u32[]{:S(2)}) %collective-permute-start.2) | collective-permute-done | bytes 1568 | tf_op jit(solution)/shard_map/ppermute | solution.py:431
  34.1 0.0 copy-start.4
  34.1 0.0 collective-permute-done.tokens
  34.1 0.6 copy-done.4
  34.7 0.0 copy-start.2
  34.7 0.7 copy-done.2
  35.4 0.0 collective-permute-done.1.out_grad
  35.5 3.3 %dispatch.3.refs_6_ = bf16[32,32,1024]{2,1,0:T(8,128)(2,1)} custom-call(bf16[192,1024]{1,0:T(8,128)(2,1)} %copy-done.2, bf16[192,1024]{1,0:T(8,128)(2,1)} %collective-permute-done.1.out_grad, s32[2,192]{1,0:T(2,128)} %copy-done.4), custom_call_target="tpu_custom_call" | custom-call | tf_op jit(solution)/shard_map/dispatch/pallas_call | solution.py:303
  38.8 2.7 %all-to-all-done = bf16[32,32,1024]{2,1,0:T(8,128)(2,1)} async-done(((bf16[32,32,1024]{2,1,0:T(8,128)(2,1)}), bf16[32,32,1024]{2,1,0:T(8,128)(2,1)}, u32[]{:S(2)}, u32[]{:S(2)}) %all-to-all-start) | async-done | bytes 2097184 | tf_op jit(solution)/shard_map/all_to_all | solution.py:435
  41.4 6.7 %all-to-all-start.1 = ((bf16[32,32,1024]{2,1,0:T(8,128)(2,1)}), bf16[32,32,1024]{2,1,0:T(8,128)(2,1)}, u32[]{:S(2)}, u32[]{:S(2)}) async-start(bf16[32,32,1024]{2,1,0:T(8,128)(2,1)} %dispatch.3.refs_6_), calls=%async_computation.1 | async-start | bytes 4194304 | tf_op jit(solution)/shard_map/all_to_all | solution.py:435
  48.2 1.4 %collective-permute-start.3 = (bf16[32,2,16,1024]{3,2,1,0:T(8,128)(2,1)}, bf16[32,2,16,1024]{3,2,1,0:T(8,128)(2,1)}, u32[]{:S(2)}, u32[]{:S(2)}) collective-permute-start(bf16[32,2,16,1024]{3,2,1,0:T(8,128)(2,1)} %bitcast.4.refs_5_), channel_id=1, source_target_pairs={{0,1},{1,2},{2,3},{3,0},{4,5},{5,6},{6,7},{7,4},{8,9},{9,10},{10,1... | collective-permute-start | bytes 6291464 | tf_op jit(solution)/shard_map/ppermute | solution.py:431
  49.6 1.5 %collective-permute-start.4 = (bf16[32,2,16,1024]{3,2,1,0:T(8,128)(2,1)}, bf16[32,2,16,1024]{3,2,1,0:T(8,128)(2,1)}, u32[]{:S(2)}, u32[]{:S(2)}) collective-permute-start(bf16[32,2,16,1024]{3,2,1,0:T(8,128)(2,1)} %bitcast.4.refs_5_), channel_id=1, source_target_pairs={{0,3},{1,0},{2,1},{3,2},{4,7},{5,4},{6,5},{7,6},{8,11},{9,8},{10,9... | collective-permute-start | bytes 6291464 | tf_op jit(solution)/shard_map/ppermute | solution.py:431
  51.1 24.0 %expert_pass.1.value = bf16[32,16,1024]{2,1,0:T(8,128)(2,1)} custom-call(s32[2]{0:T(128)} %pad_add_fusion.refs_0_, f32[32,1024]{1,0:T(8,128)} %bitcast.12, bf16[1,2816,1024]{2,1,0:T(8,128)(2,1)} %refs_2_.5, bf16[1,2816,1024]{2,1,0:T(8,128)(2,1)} %refs_3_.5, bf16[1,2816,1024]{2,1,0:T(8,128)(2,1)} %refs_4_.5, bf16[32,2,16,1024]{3,2,1,0:T(8,128)(2,1)} %bitcast.4.refs_5_, ...), custom_call_target="tpu_custom_call" | custom-call | flops 29527900160 | bytes 20447232 | tf_op jit(solution)/shard_map/expert_pass/pallas_call | solution.py:349
  75.1 1.0 all-to-all-done.1
  76.2 7.0 %all-to-all-start.2 = ((bf16[32,16,1024]{2,1,0:T(8,128)(2,1)}), bf16[32,16,1024]{2,1,0:T(8,128)(2,1)}, u32[]{:S(2)}, u32[]{:S(2)}) async-start(bf16[32,16,1024]{2,1,0:T(8,128)(2,1)} %after.1.refs_7_), calls=%async_computation.2 | async-start | bytes 2097152 | tf_op jit(solution)/shard_map/all_to_all | solution.py:435
  83.2 15.5 %weight_grads.2.after.refs_7_ = bf16[3,704,1024]{2,1,0:T(8,128)(2,1)} custom-call(s32[2]{0:T(128)} %pad_add_fusion.refs_0_, f32[32,1024]{1,0:T(8,128)} %bitcast.13, bf16[1,2816,1024]{2,1,0:T(8,128)(2,1)} %refs_2_.5, bf16[1,2816,1024]{2,1,0:T(8,128)(2,1)} %refs_3_.5, bf16[1,2816,1024]{2,1,0:T(8,128)(2,1)} %refs_4_.5, ...), custom_call_target="tpu_custom_call" | custom-call | bytes 1048576 | tf_op jit(solution)/shard_map/weight_grads/pallas_call | solution.py:401
  98.7 1.7 %all-to-all-done.2 = bf16[32,16,1024]{2,1,0:T(8,128)(2,1)} async-done(((bf16[32,16,1024]{2,1,0:T(8,128)(2,1)}), bf16[32,16,1024]{2,1,0:T(8,128)(2,1)}, u32[]{:S(2)}, u32[]{:S(2)}) %all-to-all-start.2) | async-done | bytes 1048608 | tf_op jit(solution)/shard_map/all_to_all | solution.py:435
  100.4 2.7 %combine.1 = (bf16[192,1024]{1,0:T(8,128)(2,1)}, f32[128,8,128]{2,1,0:T(8,128)}) custom-call(s32[2,192]{1,0:T(2,128)} %bitcast.17, bf16[512,1024]{1,0:T(8,128)(2,1)} %bitcast.6.back, bf16[3,704,1024]{2,1,0:T(8,128)(2,1)} %weight_grads.2.after.refs_7_), custom_call_target="tpu_custom_call" | custom-call | tf_op jit(solution)/shard_map/combine/pallas_call | solution.py:314
  103.1 8.1 %all-to-all-start.3 = ((f32[128,8,128]{2,1,0:T(8,128)}), f32[128,8,128]{2,1,0:T(8,128)}, u32[]{:S(2)}, u32[]{:S(2)}) async-start(f32[128,8,128]{2,1,0:T(8,128)} %get-tuple-element.6), calls=%async_computation.3 | async-start | bytes 1048576 | tf_op jit(solution)/shard_map/all_to_all | solution.py:435
  111.2 0.0 collective-permute-done.3.refs_5_
  111.2 0.0 collective-permute-done.4.refs_6_
  111.2 16.2 %weight_grads.3.after = bf16[3,704,1024]{2,1,0:T(8,128)(2,1)} custom-call(s32[2]{0:T(128)} %pad_add_fusion.refs_0_, f32[32,1024]{1,0:T(8,128)} %bitcast.14, bf16[1,2816,1024]{2,1,0:T(8,128)(2,1)} %refs_2_.5, bf16[1,2816,1024]{2,1,0:T(8,128)(2,1)} %refs_3_.5, bf16[1,2816,1024]{2,1,0:T(8,128)(2,1)} %refs_4_.5, ...), custom_call_target="tpu_custom_call" | custom-call | flops 14763950080 | bytes 1048576 | tf_op jit(solution)/shard_map/weight_grads/pallas_call | solution.py:401
  127.4 0.0 all-to-all-done.3.spread
  127.4 1.8 %total.1 = f32[32,1024]{1,0:T(8,128)} custom-call(f32[128,8,128]{2,1,0:T(8,128)} %all-to-all-done.3.spread, bf16[3,704,1024]{2,1,0:T(8,128)(2,1)} %weight_grads.3.after), custom_call_target="tpu_custom_call" | custom-call | tf_op jit(solution)/shard_map/total/pallas_call | solution.py:331
  (1 shorter events, 0.0 us)
Async XLA Ops:
  3.9 9.6 %copy-start = (bf16[192,1024]{1,0:T(8,128)(2,1)S(1)}, bf16[192,1024]{1,0:T(8,128)(2,1)}, u32[]{:S(2)}) copy-start(bf16[192,1024]{1,0:T(8,128)(2,1)} %tokens.1) | copy-start | bytes 1179652
  3.9 12.6 %copy-start.1 = (bf16[192,1024]{1,0:T(8,128)(2,1)S(1)}, bf16[192,1024]{1,0:T(8,128)(2,1)}, u32[]{:S(2)}) copy-start(bf16[192,1024]{1,0:T(8,128)(2,1)} %out_grad.1) | copy-start | bytes 1179652
  3.9 12.7 %copy-start.3 = (s32[192,2]{0,1:T(2,128)S(1)}, s32[192,2]{0,1:T(2,128)}, u32[]{:S(2)}) copy-start(s32[192,2]{0,1:T(2,128)} %param.9) | copy-start | bytes 4612
  3.9 37.5 %all-to-all-start = ((bf16[32,32,1024]{2,1,0:T(8,128)(2,1)}), bf16[32,32,1024]{2,1,0:T(8,128)(2,1)}, u32[]{:S(2)}, u32[]{:S(2)}) async-start(bf16[32,32,1024]{2,1,0:T(8,128)(2,1)} %dispatch.2), calls=%async_computation | async-start | bytes 4194304 | tf_op jit(solution)/shard_map/all_to_all | solution.py:435
  13.6 20.6 %collective-permute-start = (bf16[192,1024]{1,0:T(8,128)(2,1)S(1)}, bf16[192,1024]{1,0:T(8,128)(2,1)S(1)}, u32[]{:S(2)}, u32[]{:S(2)}) collective-permute-start(bf16[192,1024]{1,0:T(8,128)(2,1)S(1)} %copy-done), channel_id=1, source_target_pairs={{0,2},{1,3},{2,0},{3,1},{4,6},{5,7},{6,4},{7,5},{8,10},{9,11},{10,... | collective-permute-start | bytes 1179656 | tf_op jit(solution)/shard_map/ppermute | solution.py:431
  16.6 18.9 %collective-permute-start.1 = (bf16[192,1024]{1,0:T(8,128)(2,1)S(1)}, bf16[192,1024]{1,0:T(8,128)(2,1)}, u32[]{:S(2)}, u32[]{:S(2)}) collective-permute-start(bf16[192,1024]{1,0:T(8,128)(2,1)S(1)} %copy-done.1), channel_id=1, source_target_pairs={{0,2},{1,3},{2,0},{3,1},{4,6},{5,7},{6,4},{7,5},{8,10},{9,11},{10,... | collective-permute-start | bytes 1179656 | tf_op jit(solution)/shard_map/ppermute | solution.py:431
  16.7 17.4 %collective-permute-start.2 = (s32[2,192]{1,0:T(2,128)S(1)}, s32[2,192]{1,0:T(2,128)S(1)}, u32[]{:S(2)}, u32[]{:S(2)}) collective-permute-start(s32[2,192]{1,0:T(2,128)S(1)} %bitcast.18), channel_id=1, source_target_pairs={{0,2},{1,3},{2,0},{3,1},{4,6},{5,7},{6,4},{7,5},{8,10},{9,11},{10,... | collective-permute-start | bytes 4616 | tf_op jit(solution)/shard_map/ppermute | solution.py:431
  34.1 0.6 copy-start.4
  34.7 0.7 copy-start.2
  41.4 34.7 %all-to-all-start.1 = ((bf16[32,32,1024]{2,1,0:T(8,128)(2,1)}), bf16[32,32,1024]{2,1,0:T(8,128)(2,1)}, u32[]{:S(2)}, u32[]{:S(2)}) async-start(bf16[32,32,1024]{2,1,0:T(8,128)(2,1)} %dispatch.3.refs_6_), calls=%async_computation.1 | async-start | bytes 4194304 | tf_op jit(solution)/shard_map/all_to_all | solution.py:435
  48.2 63.0 %collective-permute-start.3 = (bf16[32,2,16,1024]{3,2,1,0:T(8,128)(2,1)}, bf16[32,2,16,1024]{3,2,1,0:T(8,128)(2,1)}, u32[]{:S(2)}, u32[]{:S(2)}) collective-permute-start(bf16[32,2,16,1024]{3,2,1,0:T(8,128)(2,1)} %bitcast.4.refs_5_), channel_id=1, source_target_pairs={{0,1},{1,2},{2,3},{3,0},{4,5},{5,6},{6,7},{7,4},{8,9},{9,10},{10,1... | collective-permute-start | bytes 6291464 | tf_op jit(solution)/shard_map/ppermute | solution.py:431
  49.6 61.6 %collective-permute-start.4 = (bf16[32,2,16,1024]{3,2,1,0:T(8,128)(2,1)}, bf16[32,2,16,1024]{3,2,1,0:T(8,128)(2,1)}, u32[]{:S(2)}, u32[]{:S(2)}) collective-permute-start(bf16[32,2,16,1024]{3,2,1,0:T(8,128)(2,1)} %bitcast.4.refs_5_), channel_id=1, source_target_pairs={{0,3},{1,0},{2,1},{3,2},{4,7},{5,4},{6,5},{7,6},{8,11},{9,8},{10,9... | collective-permute-start | bytes 6291464 | tf_op jit(solution)/shard_map/ppermute | solution.py:431
  76.2 24.2 %all-to-all-start.2 = ((bf16[32,16,1024]{2,1,0:T(8,128)(2,1)}), bf16[32,16,1024]{2,1,0:T(8,128)(2,1)}, u32[]{:S(2)}, u32[]{:S(2)}) async-start(bf16[32,16,1024]{2,1,0:T(8,128)(2,1)} %after.1.refs_7_), calls=%async_computation.2 | async-start | bytes 2097152 | tf_op jit(solution)/shard_map/all_to_all | solution.py:435
  103.1 24.3 %all-to-all-start.3 = ((f32[128,8,128]{2,1,0:T(8,128)}), f32[128,8,128]{2,1,0:T(8,128)}, u32[]{:S(2)}, u32[]{:S(2)}) async-start(f32[128,8,128]{2,1,0:T(8,128)} %get-tuple-element.6), calls=%async_computation.3 | async-start | bytes 1048576 | tf_op jit(solution)/shard_map/all_to_all | solution.py:435
